TPU v7x, 128 devices: a whole 4x4x4 slice. The times are simulated.
128 devices in a mesh: env: 8 (over x, core), wf: 16 (over y, z).
Axes of the slice: x: 4, y: 4, z: 4, core: 2. Of those that a mesh axis runs over, the one named last changes fastest.
Arguments:
- wavefunction: bfloat16 [256, 256, 256], P('wf'), may hold values from -6 to 6
- left_env: bfloat16 [32, 256, 256, 256], P('env', 'wf'), may hold values from -0.375 to 0.375
- right_env: bfloat16 [32, 256, 256, 256], P('env', 'wf'), may hold values from -0.0625 to 0.0625
- term_class: int32 [32], P('env'), may hold values from 0 to 4
- sector_sizes: int32 [2, 256], P(None, 'wf'), may hold values from 128 to 256, as said below
- source_table: int32 [5, 256], replicated, may hold values from 0 to 255, as said below
Outputs:
- product_wf: bfloat16 [256, 256, 256], P(('wf', 'env'))
Inputs may be any that keep to these rules, and one draw needn't show every extreme that they name: `sector_sizes`: both rows reach 128 and 256 on some sector. `source_table`: each row is a permutation of the 256 sectors. Sectors lie in order, 16 to an index of wf; for every class, the 16 target sectors of one index of wf are reached from exactly one sector of each index of wf.
All inputs are finite; a program needn't handle non-finite values.
Results may differ from a plain program's by a relative error of at most 0.0049.
Values may be sent and summed in bfloat16 or wider, within the bound.
A program may use at most 128 MiB of HBM per device.

v0:
```python
import jax
import jax.numpy as jnp
from jax import lax
from jax.sharding import PartitionSpec as P


def shards(wavefunction, left_env, right_env, term_class, sector_sizes, source_table):
    per_device = wavefunction.shape[0]
    block_size = wavefunction.shape[1]
    wf_index = lax.axis_index("wf")
    positions = jnp.arange(block_size)
    rows_ok = positions[None, :] < sector_sizes[0][:, None]
    cols_ok = positions[None, :] < sector_sizes[1][:, None]
    valid_mask = rows_ok[:, :, None] & cols_ok[:, None, :]
    masked = jnp.where(valid_mask, wavefunction, jnp.zeros((), wavefunction.dtype))
    wanted_all = jnp.take(source_table, term_class, axis=0)
    wanted = lax.dynamic_slice_in_dim(wanted_all, wf_index * per_device, per_device, 1)
    gathered = lax.all_gather(masked, "wf", axis=0, tiled=True)
    fetched = jnp.take(gathered, wanted.reshape(-1), axis=0)
    fetched = fetched.reshape(term_class.shape[0], per_device, block_size, block_size)
    partial_left = jnp.einsum(
        "ksab,ksbc->ksac", left_env, fetched, preferred_element_type=jnp.float32
    ).astype(jnp.bfloat16)
    combined = jnp.einsum(
        "ksac,ksdc->sad", partial_left, right_env, preferred_element_type=jnp.float32
    )
    summed = lax.psum_scatter(
        jnp.where(valid_mask, combined, jnp.zeros((), jnp.float32)),
        "env",
        scatter_dimension=0,
        tiled=True,
    )
    return summed.astype(jnp.bfloat16)


def solution(mesh):
    placed = (
        P("wf", None, None),
        P("env", "wf", None, None),
        P("env", "wf", None, None),
        P("env"),
        P(None, "wf"),
        P(),
    )
    return jax.shard_map(
        shards, mesh=mesh, in_specs=placed, out_specs=P(("wf", "env"), None, None), check_vma=False
    )
```

profile of v0, /device:TPU:1, one launch (start us, length us, event | category | flops | bytes accessed | tf_op | source)
XLA Modules:
  0.0 274.3 jit_solution(7388023332252853220)
XLA Ops:
  6.5 0.0 copy-start
  6.5 0.0 all-gather.2.cloned.1.call-start
  6.5 0.8 slice_bitcast_fusion.1
  7.3 0.1 iota_compare_fusion
  7.4 3.1 %and_select_fusion.1 = bf16[16,256,256]{2,1,0:T(8,128)(2,1)} fusion(bf16[16,256,256]{2,1,0:T(8,128)(2,1)} %param.6, pred[16,256]{1,0:T(8,128)(4,1)S(1)} %get-tuple-element.9, pred[16,256]{1,0:T(8,128)(4,1)S(1)} %get-tuple-element.10), kind=kLoop, calls=%fused_computation.11 | loop fusion | flops 2097152 | bytes 4202496 | tf_op jit(solution)/shard_map/jit(_where)/select_n | solution.py:15
  10.5 0.0 all-gather.2.cloned.1.call-update
  10.5 0.0 reduce-scatter.2.cloned.1.call-start
  10.6 0.7 compare_select_fusion.2
  11.2 0.0 copy-done
  11.3 0.6 gather_fusion
  11.8 0.7 compare_and_fusion.1
  12.5 0.1 compare_and_fusion
  12.6 0.1 reshape.89
  12.7 198.4 %all-gather.2.cloned.1.call-done = bf16[256,256,256]{2,1,0:T(8,128)(2,1)} async-done(((bf16[16,256,256]{2,1,0:T(8,128)(2,1)}), bf16[256,256,256]{2,1,0:T(8,128)(2,1)}) %all-gather.2.cloned.1.call-update) | async-done | bytes 33554448 | tf_op jit(solution)/shard_map/all_gather | solution.py:18
  211.1 7.6 %gather_fusion.1 = bf16[64,256,256]{2,1,0:T(8,128)(2,1)} fusion(bf16[256,256,256]{2,1,0:T(8,128)(2,1)} %all-gather.2.cloned.1.call-done, s32[1024]{0:T(1024)S(1)} %pad_clamp_fusion), kind=kCustom, calls=%fused_computation.1 | custom fusion | bytes 16777472 | tf_op jit(solution)/shard_map/jit(_take)/gather | solution.py:19
  218.7 0.0 copy-start.1
  218.7 12.3 %and_select_fusion = f32[16,256,256]{2,1,0:T(8,128)} fusion(pred[16,256]{1,0:T(8,128)(4,1)S(1)} %get-tuple-element.9, pred[16,256]{1,0:T(8,128)(4,1)S(1)} %get-tuple-element.10, bf16[4,16,256,256]{3,2,1,0:T(8,128)(2,1)} %param.8, bf16[4,16,256,256]{3,2,1,0:T(8,128)(2,1)} %param.7, bf16[4,16,256,256]{3,2,1,0:T(8,128)(2,1)} %bitcast.15, ...), kind=kOutput, calls=%fused_computation.10 | convolution fusion | flops 4305453056 | bytes 29368384 | tf_op jit(solution)/shard_map/ksac,ksdc->sad/dot_general | solution.py:24
  231.0 0.0 reduce-scatter.2.cloned.1.call-update
  231.0 34.7 %reduce-scatter.2.cloned.1.call-done = f32[2,256,256]{2,1,0:T(8,128)} async-done(((f32[16,256,256]{2,1,0:T(8,128)}), f32[2,256,256]{2,1,0:T(8,128)}) %reduce-scatter.2.cloned.1.call-update) | async-done | bytes 524304 | tf_op jit(solution)/shard_map/reduce_scatter | solution.py:27
  265.7 1.8 convert_element_type.11
  267.4 0.0 copy-done.1
  (3 shorter events, 0.0 us)
Async XLA Ops:
  6.5 4.7 %copy-start = (s32[5,256]{1,0:T(8,128)S(1)}, s32[5,256]{1,0:T(8,128)}, u32[]{:S(2)}) copy-start(s32[5,256]{1,0:T(8,128)} %param.11) | copy-start | bytes 15364
  6.5 204.6 %all-gather.2.cloned.1.call-start = ((), (), s32[]{:S(2)}) async-start(), calls=%async_computation.1 | async-start | bytes 35651584 | tf_op jit(solution)/shard_map/all_gather | solution.py:18
  10.5 255.1 %reduce-scatter.2.cloned.1.call-start = ((), (), s32[]{:S(2)}) async-start(), calls=%async_computation.2 | async-start | bytes 4718592 | tf_op jit(solution)/shard_map/reduce_scatter | solution.py:27
  218.7 48.7 %copy-start.1 = (s32[5,256]{1,0:T(8,128)S(1)}, s32[5,256]{1,0:T(8,128)}, u32[]{:S(2)}) copy-start(s32[5,256]{1,0:T(8,128)} %param.11) | copy-start | bytes 15364
Sparse Core Ops, SparseCore 0:
  10.6 200.4 all-gather.1
  231.1 34.4 reduce-scatter.1
where the time goes:
time: 277 us; the launch traced here: 274 us
  waiting for transfers between devices  233 us (84%)
  between operations  13.4 us (5%)
  matrix products  12.3 us (4%)
  local copies, waits for them, and re-layouts  9.04 us (3%)
  other arithmetic  6.4 us (2%)
    all_gather x1, waiting for transfers between devices, shards(): gathered = lax.all_gather(masked, 'wf', axis=0, tiled=True)  198 us
    reduce_scatter x1, waiting for transfers between devices, shards(): lax.psum_scatter(jnp.where(valid_mask, combined, jnp.zeros((), jnp.float3...  34.7 us
    dot_general x1, matrix products, shards(): jnp.einsum('ksac,ksdc->sad', partial_left, right_env, preferred_element_t...  12.3 us
    gather x1, local copies, waits for them, and re-layouts, shards(): fetched = jnp.take(gathered, wanted.reshape(-1), axis=0)  7.63 us
  transfers between devices with their start and end apart: 2, of which 2 were waited for; matrix products, arithmetic and copies ran while one was open for 1% of the time, Pallas kernels for 0%

commit v1 on v0

v1 whole, which is shorter than its diff:
```python
import jax
import jax.numpy as jnp
from jax import lax
from jax.experimental import pallas as pl
from jax.experimental.pallas import tpu as pltpu
from jax.sharding import PartitionSpec as P

MESH = pl.DeviceIdType.MESH
B = 256
HALF = B // 2
PIECE = HALF // 4
CLASSES = 5
GROUP = 16
TERMS = 4

COOP = (
    ((1, 1), (1, 0)),
    ((3, 3), (3, 0)),
    ((1, 3), (0, 3)),
    ((3, 1), (0, 1)),
    ((2, 1), (0, 1)),
    ((2, 3), (0, 3)),
    ((1, 2), (1, 0)),
    ((3, 2), (3, 0)),
    ((2, 2), None),
)
DIRECT = ((0, 1), (0, 3), (1, 0), (3, 0), (0, 2), (2, 0))
OFFSETS = tuple(o for o, _ in COOP) + DIRECT
NC, ND, NO = len(COOP), len(DIRECT), len(COOP) + len(DIRECT)
XORDER = (2, 1, 3, 0)


def body(slot, qinv, osrc, klass, sizes, wf_hbm, left_hbm, right_hbm, out, *scratch):
    recv = scratch[:NO]
    (wf, left, right, stage_c, transit, stage_d, partial, core_out, core_in, mine, x_out, x_in,
     load_sem, s1, r1, s2, r2, sd, rd, sx, rx, sf, rf, sc, rc, sp, rp, sr, rr) = scratch[NO:]
    e, w = lax.axis_index("env"), lax.axis_index("wf")
    x, c, y, z = e // 2, e % 2, w // 4, w % 4

    def dev(dx, dc, dy, dz):
        return (((x + dx) % 4) * 2 + (c + dc) % 2, ((y + dy) % 4) * 4 + (z + dz) % 4)

    def remote(src, dst, ssem, rsem, dx, dc, dy, dz):
        return pltpu.make_async_remote_copy(
            src_ref=src, dst_ref=dst, send_sem=ssem, recv_sem=rsem, device_id=dev(dx, dc, dy, dz), device_id_type=MESH)

    load_wf = pltpu.make_async_copy(wf_hbm, wf, load_sem.at[0])
    load_wf.start()
    barrier = pltpu.get_barrier_semaphore()
    partners = [(0, 1, 0, 0)] + [(d, 0, 0, 0) for d in (1, 2, 3)] + [(0, 0, d, 0) for d in (1, 2, 3)] + [(0, 0, 0, d) for d in (1, 2, 3)]
    for p in partners:
        pl.semaphore_signal(barrier, inc=1, device_id=dev(*p), device_id_type=MESH)
    load_wf.wait()
    load_left = pltpu.make_async_copy(left_hbm, left, load_sem.at[1])
    load_right = pltpu.make_async_copy(right_hbm, right, load_sem.at[2])
    load_left.start()
    load_right.start()

    rows = lax.broadcasted_iota(jnp.int32, (B, B), 0)
    cols = lax.broadcasted_iota(jnp.int32, (B, B), 1)

    @pl.loop(0, GROUP)
    def _(q):
        keep = (rows < sizes[0, q]) & (cols < sizes[1, q])
        wf[q] = jnp.where(keep, wf[q].astype(jnp.float32), 0.0).astype(jnp.bfloat16)

    half = pl.multiple_of(c * HALF, HALF)
    piece = pl.multiple_of(c * HALF + x * PIECE, PIECE)
    prev_piece = pl.multiple_of(c * HALF + ((x + 3) % 4) * PIECE, PIECE)
    next_piece = pl.multiple_of(c * HALF + ((x + 1) % 4) * PIECE, PIECE)
    low = PIECE // 2

    def target(o):
        return ((y + o[0]) % 4) * 4 + (z + o[1]) % 4

    def stage(dst, o, first, count):
        @pl.loop(0, CLASSES)
        def _(k):
            dst[k] = wf[slot[k, target(o)], pl.ds(first, count)]

    def leg1(i):
        o, hop = COOP[i]
        if hop is None:
            hop = (2 * (1 - c), 2 * c)
        return remote(stage_c.at[i], transit.at[i], s1.at[i], r1.at[i], 0, 0, *hop)

    def leg2(i):
        o, hop = COOP[i]
        hop = (2 * c, 2 * (1 - c)) if hop is None else ((o[0] - hop[0]) % 4, (o[1] - hop[1]) % 4)
        return remote(transit.at[i], recv[i].at[:, pl.ds(piece, PIECE)], s2.at[i], r2.at[i], 0, 0, *hop)

    def direct(i):
        return remote(stage_d.at[i], recv[NC + i].at[:, pl.ds(half, HALF)], sd.at[i], rd.at[i], 0, 0, *DIRECT[i])

    def share(i, side):
        part = recv[i].at[:, pl.ds(piece, PIECE)]
        return remote(part, part, sx.at[side, i], rx.at[side, i], 1 if side == 0 else 3, 0, 0, 0)

    def forward(i, side):
        first = prev_piece if side == 0 else next_piece + low
        part = recv[i].at[:, pl.ds(pl.multiple_of(first, low), low)]
        return remote(part, part, sf.at[side, i], rf.at[side, i], 1 if side == 0 else 3, 0, 0, 0)

    def across(i):
        part = recv[i].at[:, pl.ds(half, HALF)]
        return remote(part, part, sc.at[i], rc.at[i], 0, 1, 0, 0)

    def first_product(i):
        o = OFFSETS[i]

        @pl.loop(0, TERMS)
        def _(k):
            kind = klass[k]
            at = o[0] * 4 + o[1]
            got = lax.dot_general(left[k, qinv[kind, at]], recv[i][kind], (((1,), (0,)), ((), ())), preferred_element_type=jnp.float32)
            partial[k, at] = got.astype(jnp.bfloat16)

    for i in range(NC):
        stage(stage_c.at[i], COOP[i][0], piece, PIECE)
    pl.semaphore_wait(barrier, len(partners))
    for i in range(NC):
        leg1(i).start()
    for i in range(ND):
        stage(stage_d.at[i], DIRECT[i], half, HALF)

    for i in range(4):
        leg1(i).wait_recv()
        leg2(i).start()
    for i in range(4):
        direct(i).start()
    for i in range(4, NC):
        leg1(i).wait_recv()
        leg2(i).start()
    for i in range(4, ND):
        direct(i).start()

    load_left.wait()

    @pl.loop(0, TERMS)
    def _(k):
        kind = klass[k]
        got = lax.dot_general(left[k, qinv[kind, 0]], wf[slot[kind, target((0, 0))]], (((1,), (0,)), ((), ())), preferred_element_type=jnp.float32)
        partial[k, 0] = got.astype(jnp.bfloat16)

    def step_share(i):
        leg2(i).wait_recv()
        share(i, 0).start()
        share(i, 1).start()

    def step_forward(i):
        for side in (0, 1):
            share(i, side).wait_recv()
            forward(i, side).start()

    def step_across(i):
        for side in (0, 1):
            forward(i, side).wait_recv()
        across(i).start()

    def step_direct(i):
        direct(i).wait_recv()
        across(NC + i).start()

    def step_product(i):
        across(i).wait_recv()
        first_product(i)

    for t in range(NC + 4):
        if t < NC:
            step_share(t)
        if 0 <= t - 1 < NC:
            step_forward(t - 1)
        if 0 <= t - 2 < NC:
            step_across(t - 2)
        if 0 <= t - 4 < NC:
            step_product(t - 4)
        if 0 <= t - 5 < ND:
            step_direct(t - 5)
        if 0 <= t - 7 < ND:
            step_product(NC + t - 7)
    load_right.wait()

    def second_product(q):
        total = jnp.zeros((B, B), jnp.float32)
        for k in range(TERMS):
            total += lax.dot_general(partial[k, osrc[klass[k], q]], right[k, q], (((1,), (1,)), ((), ())), preferred_element_type=jnp.float32)
        return total

    def to_core(n):
        return remote(core_out.at[n], core_in.at[n], sp.at[n], rp.at[n], 0, 1, 0, 0)

    def to_plane(n):
        return remote(x_out.at[n], x_in.at[n], sr.at[n], rr.at[n], XORDER[n], 0, 0, 0)

    def theirs(n):
        first = ((x + XORDER[n]) % 4) * 4 + 2 * (1 - c)

        @pl.loop(0, 2)
        def _(j):
            core_out[n, j] = second_product(first + j)

        to_core(n).start()

    def ours(n):
        first = ((x + XORDER[n]) % 4) * 4 + 2 * c

        @pl.loop(0, 2)
        def _(j):
            mine[n, j] = second_product(first + j)

    def send_sum(n):
        to_core(n).wait_recv()

        @pl.loop(0, 2)
        def _(j):
            x_out[n, j] = (mine[n, j] + core_in[n, j]).astype(jnp.bfloat16)

        to_plane(n).start()

    theirs(0)
    theirs(1)
    ours(0)
    send_sum(0)
    ours(1)
    send_sum(1)
    theirs(2)
    theirs(3)
    ours(2)
    send_sum(2)
    ours(3)
    to_core(3).wait_recv()
    for n in (1, 2, 0):
        to_plane(n).wait_recv()

    @pl.loop(0, 2)
    def _(j):
        q = 4 * x + 2 * c + j
        total = mine[3, j] + core_in[3, j]
        for n in range(3):
            total += x_in[n, j].astype(jnp.float32)
        keep = (rows < sizes[0, q]) & (cols < sizes[1, q])
        out[j] = jnp.where(keep, total, 0.0).astype(jnp.bfloat16)

    for i in range(NC):
        leg1(i).wait_send()
        leg2(i).wait_send()
        for side in (0, 1):
            share(i, side).wait_send()
            forward(i, side).wait_send()
    for i in range(ND):
        direct(i).wait_send()
    for i in range(NO):
        across(i).wait_send()
    for n in range(4):
        to_core(n).wait_send()
    for n in range(3):
        to_plane(n).wait_send()


def shards(wavefunction, left_env, right_env, term_class, sector_sizes, source_table):
    w = lax.axis_index("wf")
    y, z = w // 4, w % 4
    groups = jnp.arange(GROUP, dtype=jnp.int32)
    blocks = source_table.reshape(CLASSES, GROUP, GROUP)
    slot = jnp.sum(jnp.where(blocks // GROUP == w, blocks % GROUP, 0), axis=2)
    here = lax.dynamic_slice_in_dim(source_table, w * GROUP, GROUP, 1) // GROUP
    osrc = ((y - here // 4) % 4) * 4 + (z - here % 4) % 4
    qinv = jnp.sum(jnp.where(osrc[:, None, :] == groups[None, :, None], groups[None, None, :], 0), axis=2)
    bf16, f32, dma = jnp.bfloat16, jnp.float32, pltpu.SemaphoreType.DMA
    smem = pl.BlockSpec(memory_space=pltpu.SMEM)
    anywhere = pl.BlockSpec(memory_space=pl.ANY)
    return pl.pallas_call(
        body,
        out_shape=jax.ShapeDtypeStruct((2, B, B), bf16),
        in_specs=[smem] * 5 + [anywhere] * 3,
        out_specs=pl.BlockSpec(memory_space=pltpu.VMEM),
        scratch_shapes=[pltpu.VMEM((CLASSES, B, B), bf16)] * NO + [
            pltpu.VMEM((GROUP, B, B), bf16),
            pltpu.VMEM((TERMS, GROUP, B, B), bf16),
            pltpu.VMEM((TERMS, GROUP, B, B), bf16),
            pltpu.VMEM((NC, CLASSES, PIECE, B), bf16),
            pltpu.VMEM((NC, CLASSES, PIECE, B), bf16),
            pltpu.VMEM((ND, CLASSES, HALF, B), bf16),
            pltpu.VMEM((TERMS, GROUP, B, B), bf16),
            pltpu.VMEM((4, 2, B, B), f32),
            pltpu.VMEM((4, 2, B, B), f32),
            pltpu.VMEM((4, 2, B, B), f32),
            pltpu.VMEM((3, 2, B, B), bf16),
            pltpu.VMEM((3, 2, B, B), bf16),
            dma((3,)), dma((NC,)), dma((NC,)), dma((NC,)), dma((NC,)), dma((ND,)), dma((ND,)),
            dma((2, NC)), dma((2, NC)), dma((2, NC)), dma((2, NC)), dma((NO,)), dma((NO,)),
            dma((4,)), dma((4,)), dma((3,)), dma((3,)),
        ],
        compiler_params=pltpu.CompilerParams(collective_id=0, has_side_effects=True, vmem_limit_bytes=56 * 2**20),
        cost_estimate=pl.CostEstimate(flops=2 * 2 * TERMS * GROUP * B**3, bytes_accessed=2 * (2 * TERMS + 1) * GROUP * B * B, transcendentals=0),
        name="fetch_multiply_reduce",
    )(slot, qinv, osrc, term_class, sector_sizes, wavefunction, left_env, right_env)


def solution(mesh):
    placed = (
        P("wf", None, None),
        P("env", "wf", None, None),
        P("env", "wf", None, None),
        P("env"),
        P(None, "wf"),
        P(),
    )
    return jax.shard_map(
        shards, mesh=mesh, in_specs=placed, out_specs=P(("wf", "env"), None, None), check_vma=False
    )
```

time: 277 us -> 78.6 us (0.28)
  waiting for transfers between devices: 233 us -> 0 us
  Pallas kernels: 0 us -> 74.2 us
  between operations: 13.4 us -> 0.02 us
  matrix products: 12.3 us -> 0 us
  local copies, waits for them, and re-layouts: 9.04 us -> 2.45 us
  other arithmetic: 6.4 us -> 1.64 us
    all_gather x1 -> x0, waiting for transfers between devices: 198 us -> none  [shards(): gathered = lax.all_gather(masked, 'wf', axis=0, tiled=True)]
    pallas_call x0 -> x1, Pallas kernels: none -> 74.2 us  [shards(): pl.pallas_call(body, out_shape=jax.ShapeDtypeStruct((2, B, B), bf16), in_...]
    reduce_scatter x1 -> x0, waiting for transfers between devices: 34.7 us -> none  [shards(): lax.psum_scatter(jnp.where(valid_mask, combined, jnp.zeros((), jnp.float3...]
    dot_general x1 -> x0, matrix products: 12.3 us -> none  [shards(): jnp.einsum('ksac,ksdc->sad', partial_left, right_env, preferred_element_t...]
    gather x2 -> x0, local copies, waits for them, and re-layouts: 8.19 us -> none  [the longest x1 7.63 us: shards(): fetched = jnp.take(gathered, wanted.reshape(-1), axis=0)]
    select_n x3 -> x0, other arithmetic: 3.79 us -> none  [the longest x1 3.12 us: shards(): jnp.where(valid_mask, wavefunction, jnp.zeros((), wavefunction.dtype))]
  transfers between devices with their start and end apart: 2 -> 0, of which waited for: 2 -> 0; matrix products, arithmetic and copies ran while one was open for 1% -> 0% of each run, Pallas kernels for 0% -> 0%
where the time goes in v1:
time: 78.6 us; the launch traced here: 78.3 us
  Pallas kernels  74.2 us (94%)
  local copies, waits for them, and re-layouts  2.45 us (3%)
  other arithmetic  1.64 us (2%)
    pallas_call x1, Pallas kernels, shards(): pl.pallas_call(body, out_shape=jax.ShapeDtypeStruct((2, B, B), bf16), in_...  74.2 us
    unnamed x3, local copies, waits for them, and re-layouts  1.67 us

profile of v1, /device:TPU:1, one launch (start us, length us, event | category | flops | bytes accessed | tf_op | source)
XLA Modules:
  0.0 78.3 jit_solution(13047085169788864323)
XLA Ops:
  0.0 0.8 fusion.9.osrc
  0.8 0.0 copy-start
  0.8 0.8 reshape.4
  1.6 0.9 %fusion.2 = (s32[5,16]{1,0:T(8,128)}, s32[5,16]{1,0:T(8,128)}) fusion(s32[5,16,16]{2,1,0:T(8,128)S(1)} %reshape.4, s32[]{:T(128)S(6)} %axis_index.12, s32[5,16]{1,0:T(8,128)S(1)} %fusion.9.osrc), kind=kLoop, calls=%fused_computation.7 | loop fusion | flops 31840 | bytes 6084 | tf_op jit(solution)/shard_map/reduce_sum | solution.py:265
  2.4 0.0 copy-done
  2.4 74.2 %fetch_multiply_reduce.1 = bf16[2,256,256]{2,1,0:T(8,128)(2,1)} custom-call(s32[5,16]{1,0:T(8,128)} %get-tuple-element.5.slot, s32[5,16]{1,0:T(8,128)} %get-tuple-element.6.qinv, s32[5,16]{1,0:T(8,128)} %copy-done, s32[4]{0:T(128)} %klass.1, s32[2,16]{1,0:T(2,128)} %sizes.1, bf16[16,256,256]{2,1,0:T(8,128)(2,1)} %wf_hbm.1, ...), custom_call_target="tpu_custom_call" | custom-call | flops 4294967296 | bytes 18874368 | tf_op jit(solution)/shard_map/fetch_multiply_reduce/pallas_call | solution.py:272
  76.6 1.7 %copy.8 = bf16[2,256,256]{2,1,0:T(8,128)(2,1)} copy(bf16[2,256,256]{2,1,0:T(8,128)(2,1)} %fetch_multiply_reduce.1) | data formatting | bytes 524288
Async XLA Ops:
  0.8 1.6 %copy-start = (s32[5,16]{1,0:T(8,128)}, s32[5,16]{1,0:T(8,128)S(1)}, u32[]{:S(2)}) copy-start(s32[5,16]{1,0:T(8,128)S(1)} %fusion.9.osrc) | copy-start | bytes 964

commit v2 on v0

v2 whole, which is shorter than its diff:
```python
import jax
import jax.numpy as jnp
from jax import lax
from jax.experimental import pallas as pl
from jax.experimental.pallas import tpu as pltpu
from jax.sharding import PartitionSpec as P

MESH = pl.DeviceIdType.MESH
B = 256
HALF = B // 2
PIECE = HALF // 4
CLASSES = 5
GROUP = 16
TERMS = 4
CHIP = 2 * TERMS

COOP = ((1, 1), (3, 3), (1, 3), (3, 1), (2, 1), (2, 3), (1, 2), (3, 2), (2, 2))
DIRECT = ((0, 1), (0, 3), (1, 0), (3, 0), (0, 2), (2, 0))
OFFSETS = COOP + DIRECT + ((0, 0),)
NC, ND, NO = len(COOP), len(DIRECT), len(COOP) + len(DIRECT)
UNROLL = 8
ORDER = (
    "L0", "L1", "L2", "L3", "L4", "L5", "L6", "L7", "L8", "X0", "T0", "T1", "T2", "T3", "T4", "T5", "D0", "D1", "D2",
    "D3", "D4", "D5", "S0", "S1", "S2", "S3", "F0", "F1", "S4", "A0", "S5", "F2", "A1", "S6", "F3", "A2", "O0", "P0",
    "F4", "S7", "A3", "P1", "F5", "S8", "A4", "E0", "P2", "F6", "A5", "E1", "P3", "P4", "F7", "A6", "E2", "E3", "P5",
    "P9", "F8", "A7", "P6", "P10", "A8", "E4", "E5", "P7", "P11", "P12", "P13", "P14", "P8",
)


def body(index, klass, sizes, wf_hbm, left_hbm, right_hbm, out, *scratch):
    recv = scratch[:NO + 1]
    (wf, left, right, stage_c, stage_d, partial, kept, via_out, via_in, x_out, x_in, kinds_out, kinds_in, kinds,
     load_sem, ss, rs, sq, rq, sd, rd, sx, rx, sf, rf, sc, rc, sv, rv, sr, rr) = scratch[NO + 1:]
    e, w = lax.axis_index("env"), lax.axis_index("wf")
    x, c, y, z = e // 2, e % 2, w // 4, w % 4

    def dev(dx, dc, dy, dz):
        return (((x + dx) % 4) * 2 + (c + dc) % 2, ((y + dy) % 4) * 4 + (z + dz) % 4)

    def remote(src, dst, ssem, rsem, dx, dc, dy, dz):
        return pltpu.make_async_remote_copy(
            src_ref=src, dst_ref=dst, send_sem=ssem, recv_sem=rsem, device_id=dev(dx, dc, dy, dz), device_id_type=MESH)

    load_wf = pltpu.make_async_copy(wf_hbm, wf, load_sem.at[0])
    load_wf.start()
    barrier = pltpu.get_barrier_semaphore()
    partners = [(0, 1, 0, 0), (1, 0, 0, 0), (3, 0, 0, 0)] + [(0, 0, *o) for o in COOP + DIRECT]
    for p in partners:
        pl.semaphore_signal(barrier, inc=1, device_id=dev(*p), device_id_type=MESH)
    load_wf.wait()
    own_terms = pl.ds(c * TERMS, TERMS)
    load_left = pltpu.make_async_copy(left_hbm.at[:, :, c], left.at[own_terms], load_sem.at[1])
    load_right = pltpu.make_async_copy(right_hbm.at[:, :, c], right.at[own_terms], load_sem.at[2])
    load_left.start()
    load_right.start()
    for k in range(TERMS):
        kinds_out[k] = klass[k]
        kinds[c * TERMS + k] = klass[k]

    half = pl.multiple_of(c * HALF, HALF)
    piece = pl.multiple_of(c * HALF + x * PIECE, PIECE)
    prev_piece = pl.multiple_of(c * HALF + ((x + 3) % 4) * PIECE, PIECE)
    next_piece = pl.multiple_of(c * HALF + ((x + 1) % 4) * PIECE, PIECE)
    low = PIECE // 2

    def target(o):
        return ((y + o[0]) % 4) * 4 + (z + o[1]) % 4

    def masked(value, first, q):
        rows = lax.broadcasted_iota(jnp.int32, value.shape, 0) + first
        cols = lax.broadcasted_iota(jnp.int32, value.shape, 1)
        keep = (rows < sizes[0, q]) & (cols < sizes[1, q])
        return jnp.where(keep, value.astype(jnp.float32), 0.0).astype(jnp.bfloat16)

    def stage(dst, o, first, count):
        @pl.loop(0, CLASSES)
        def _(k):
            q = index[0, k, target(o)]
            dst[k] = masked(wf[q, pl.ds(first, count)], first, q)

    def quarter(i):
        return remote(stage_c.at[i], recv[i].at[:, pl.ds(piece, PIECE)], sq.at[i], rq.at[i], 0, 0, *COOP[i])

    def direct(i):
        return remote(stage_d.at[i], recv[NC + i].at[:, pl.ds(half, HALF)], sd.at[i], rd.at[i], 0, 0, *DIRECT[i])

    def share(i, side):
        part = recv[i].at[:, pl.ds(piece, PIECE)]
        return remote(part, part, sx.at[side, i], rx.at[side, i], 1 if side == 0 else 3, 0, 0, 0)

    def forward(i, side):
        first = prev_piece if side == 0 else next_piece + low
        part = recv[i].at[:, pl.ds(pl.multiple_of(first, low), low)]
        return remote(part, part, sf.at[side, i], rf.at[side, i], 1 if side == 0 else 3, 0, 0, 0)

    def across(i):
        part = recv[i].at[:, pl.ds(half, HALF)]
        return remote(part, part, sc.at[i], rc.at[i], 0, 1, 0, 0)

    def swap_env(n):
        src, dst = ((left_hbm, left), (right_hbm, right))[n]
        return remote(src.at[:, :, 1 - c], dst.at[own_terms], ss.at[n], rs.at[n], 0, 1, 0, 0)

    def swap_kinds():
        return remote(kinds_out, kinds_in, ss.at[2], rs.at[2], 0, 1, 0, 0)

    def first_product(i):
        o = OFFSETS[i]
        at = o[0] * 4 + o[1]

        @pl.loop(0, CHIP // UNROLL)
        def _(n):
            for u in range(UNROLL):
                k = n * UNROLL + u
                q = index[1, kinds[k], at]
                got = lax.dot_general(left[k, q // 4, q % 2], recv[i][kinds[k]], (((1,), (0,)), ((), ())), preferred_element_type=jnp.float32)
                partial[k, at] = got.astype(jnp.bfloat16)

    for i in range(NC):
        stage(stage_c.at[i], COOP[i], piece, PIECE)
    pl.semaphore_wait(barrier, len(partners))
    def step_swap(i):
        swap_kinds().start()
        swap_env(0).start()
        swap_env(1).start()

    def step_stage(i):
        stage(stage_d.at[i], DIRECT[i], half, HALF)

    def step_quarter(i):
        quarter(i).start()

    def step_begin(i):
        direct(i).start()

    def step_share(i):
        quarter(i).wait_recv()
        share(i, 0).start()
        share(i, 1).start()

    def step_forward(i):
        for side in (0, 1):
            share(i, side).wait_recv()
            forward(i, side).start()

    def step_across(i):
        for side in (0, 1):
            forward(i, side).wait_recv()
        across(i).start()

    def step_direct(i):
        direct(i).wait_recv()
        across(NC + i).start()

    def step_product(i):
        across(i).wait_recv()
        first_product(i)

    def step_own(i):
        load_left.wait()
        swap_kinds().wait_recv()
        for k in range(TERMS):
            kinds[(1 - c) * TERMS + k] = kinds_in[k]
        swap_env(0).wait_recv()
        stage(recv[NO], (0, 0), 0, B)
        first_product(NO)

    steps = {"L": step_quarter, "X": step_swap, "T": step_stage, "D": step_begin, "S": step_share, "F": step_forward, "A": step_across, "E": step_direct, "P": step_product, "O": step_own}
    for step in ORDER:
        steps[step[0]](int(step[1:]))

    load_right.wait()
    swap_env(1).wait_recv()

    def second_product(g, j):
        q = 4 * g + 2 * c + j
        total = jnp.zeros((B, B), jnp.float32)
        for k in range(CHIP):
            total += lax.dot_general(partial[k, index[2, kinds[k], q]], right[k, g, j], (((1,), (1,)), ((), ())), preferred_element_type=jnp.float32)
        return total

    def via(n):
        return remote(via_out.at[n], via_in.at[n], sv.at[n], rv.at[n], (1, 3)[n], 0, 0, 0)

    def to_plane(n, j):
        return remote(x_out.at[n, j], x_in.at[n, j], sr.at[n, j], rr.at[n, j], (1, 3)[n], 0, 0, 0)

    for n in range(2):
        via_out[n] = second_product((x + 2) % 4, n).astype(jnp.bfloat16)
        via(n).start()
    for n in range(2):
        x_out[n, 1 - n] = second_product((x + (1, 3)[n]) % 4, 1 - n).astype(jnp.bfloat16)
        to_plane(n, 1 - n).start()
    for n in range(2):
        kept[n] = second_product((x + (1, 3)[n]) % 4, n)
    for n in range(2):
        via(n).wait_recv()
        x_out[n, n] = (kept[n] + via_in[n].astype(jnp.float32)).astype(jnp.bfloat16)
        to_plane(n, n).start()
    for j in range(2):
        kept[2 + j] = second_product(x, j)
    for j in range(2):
        total = kept[2 + j]
        for n in (1 - j, j):
            to_plane(n, j).wait_recv()
            total += x_in[n, j].astype(jnp.float32)
        out[j] = masked(total, 0, 4 * x + 2 * c + j)

    for i in range(NC):
        quarter(i).wait_send()
        for side in (0, 1):
            share(i, side).wait_send()
            forward(i, side).wait_send()
    for i in range(ND):
        direct(i).wait_send()
    for i in range(NO):
        across(i).wait_send()
    for n in range(2):
        swap_env(n).wait_send()
    swap_kinds().wait_send()
    for n in range(2):
        via(n).wait_send()
        for j in range(2):
            to_plane(n, j).wait_send()


def shards(wavefunction, left_env, right_env, term_class, sector_sizes, source_table):
    w = lax.axis_index("wf")
    y, z = w // 4, w % 4
    shape = (3, CLASSES, GROUP, GROUP * GROUP)
    what, at, sector = (lax.broadcasted_iota(jnp.int32, shape, n) for n in (0, 2, 3))
    offset = ((y - source_table // 64) % 4) * 4 + (z - source_table // GROUP % 4) % 4
    code = (offset * GROUP + source_table % GROUP)[None, :, None, :]
    offset, place = code // GROUP, code % GROUP
    group, member = sector // GROUP, sector % GROUP
    which = jnp.where(what == 0, (group == at) & (offset == 0), (group == w) & (at == jnp.where(what == 1, offset, member)))
    value = jnp.where(what == 0, place, jnp.where(what == 1, member, offset))
    index = jnp.sum(jnp.where(which, value, 0), axis=3)

    def by_core(env):
        return env.reshape(TERMS, 4, 2, 2, B, B)

    bf16, f32, dma = jnp.bfloat16, jnp.float32, pltpu.SemaphoreType.DMA
    smem = pl.BlockSpec(memory_space=pltpu.SMEM)
    anywhere = pl.BlockSpec(memory_space=pl.ANY)
    return pl.pallas_call(
        body,
        out_shape=jax.ShapeDtypeStruct((2, B, B), bf16),
        in_specs=[smem] * 3 + [anywhere] * 3,
        out_specs=pl.BlockSpec(memory_space=pltpu.VMEM),
        scratch_shapes=[pltpu.VMEM((CLASSES, B, B), bf16)] * (NO + 1) + [
            pltpu.VMEM((GROUP, B, B), bf16),
            pltpu.VMEM((CHIP, 4, 2, B, B), bf16),
            pltpu.VMEM((CHIP, 4, 2, B, B), bf16),
            pltpu.VMEM((NC, CLASSES, PIECE, B), bf16),
            pltpu.VMEM((ND, CLASSES, HALF, B), bf16),
            pltpu.VMEM((CHIP, GROUP, B, B), bf16),
            pltpu.VMEM((4, B, B), f32),
            pltpu.VMEM((2, B, B), bf16),
            pltpu.VMEM((2, B, B), bf16),
            pltpu.VMEM((2, 2, B, B), bf16),
            pltpu.VMEM((2, 2, B, B), bf16),
            pltpu.SMEM((TERMS,), jnp.int32), pltpu.SMEM((TERMS,), jnp.int32), pltpu.SMEM((CHIP,), jnp.int32),
            dma((3,)), dma((3,)), dma((3,)), dma((NC,)), dma((NC,)), dma((ND,)), dma((ND,)),
            dma((2, NC)), dma((2, NC)), dma((2, NC)), dma((2, NC)), dma((NO,)), dma((NO,)),
            dma((2,)), dma((2,)), dma((2, 2)), dma((2, 2)),
        ],
        compiler_params=pltpu.CompilerParams(collective_id=0, has_side_effects=True, vmem_limit_bytes=60 * 2**20),
        cost_estimate=pl.CostEstimate(flops=2 * 2 * TERMS * GROUP * B**3, bytes_accessed=2 * (2 * TERMS + 1) * GROUP * B * B, transcendentals=0),
        name="fetch_multiply_reduce",
    )(index, term_class, sector_sizes, wavefunction, by_core(left_env), by_core(right_env))


def solution(mesh):
    placed = (
        P("wf", None, None),
        P("env", "wf", None, None),
        P("env", "wf", None, None),
        P("env"),
        P(None, "wf"),
        P(),
    )
    return jax.shard_map(
        shards, mesh=mesh, in_specs=placed, out_specs=P(("wf", "env"), None, None), check_vma=False
    )
```

time: 277 us -> 65.7 us (0.24)
  waiting for transfers between devices: 233 us -> 0 us
  Pallas kernels: 0 us -> 61.9 us
  between operations: 13.4 us -> 0.03 us
  matrix products: 12.3 us -> 0 us
  local copies, waits for them, and re-layouts: 9.04 us -> 1.67 us
  other arithmetic: 6.4 us -> 1.8 us
    all_gather x1 -> x0, waiting for transfers between devices: 198 us -> none  [shards(): gathered = lax.all_gather(masked, 'wf', axis=0, tiled=True)]
    pallas_call x0 -> x1, Pallas kernels: none -> 61.9 us  [shards(): pl.pallas_call(body, out_shape=jax.ShapeDtypeStruct((2, B, B), bf16), in_...]
    reduce_scatter x1 -> x0, waiting for transfers between devices: 34.7 us -> none  [shards(): lax.psum_scatter(jnp.where(valid_mask, combined, jnp.zeros((), jnp.float3...]
    dot_general x1 -> x0, matrix products: 12.3 us -> none  [shards(): jnp.einsum('ksac,ksdc->sad', partial_left, right_env, preferred_element_t...]
    gather x2 -> x0, local copies, waits for them, and re-layouts: 8.19 us -> none  [the longest x1 7.63 us: shards(): fetched = jnp.take(gathered, wanted.reshape(-1), axis=0)]
    select_n x3 -> x1, other arithmetic: 3.79 us -> 0.01 us  [shards(): offset, place = (code // GROUP, code % GROUP)]
  transfers between devices with their start and end apart: 2 -> 0, of which waited for: 2 -> 0; matrix products, arithmetic and copies ran while one was open for 1% -> 0% of each run, Pallas kernels for 0% -> 0%
where the time goes in v2:
time: 65.7 us; the launch traced here: 65.4 us
  Pallas kernels  61.9 us (94%)
  other arithmetic  1.8 us (3%)
  local copies, waits for them, and re-layouts  1.67 us (3%)
    pallas_call x1, Pallas kernels, shards(): pl.pallas_call(body, out_shape=jax.ShapeDtypeStruct((2, B, B), bf16), in_...  61.9 us
    unnamed x1, local copies, waits for them, and re-layouts  1.67 us

profile of v2, /device:TPU:1, one launch (start us, length us, event | category | flops | bytes accessed | tf_op | source)
XLA Modules:
  0.0 65.4 jit_solution(1772905763136038342)
XLA Ops:
  0.0 0.7 %broadcast_compare_fusion = (pred[5,256]{1,0:T(8,128)(4,1)S(1)}, s32[5,256]{1,0:T(8,128)S(1)}, s32[5,256]{1,0:T(8,128)S(1)}) fusion(s32[]{:T(128)S(6)} %select_n.88, s32[5,256]{1,0:T(8,128)} %param.11, s32[]{:T(128)S(6)} %select_n.85), kind=kLoop, calls=%fused_computation.48 | loop fusion | flops 107520 | bytes 16648 | tf_op jit(solution)/shard_map/eq | solution.py:236
  0.8 1.0 %fusion.3.index = s32[3,5,16]{2,1,0:T(8,128)} fusion(s32[5,256]{1,0:T(8,128)S(1)} %add_select_fusion, s32[256]{0:T(256)S(1)} %get-tuple-element.9, s32[256]{0:T(256)S(1)} %get-tuple-element.12, s32[5,256]{1,0:T(8,128)S(1)} %get-tuple-element.6, s32[]{:T(128)S(6)} %axis_index.12, s32[256]{0:T(256)S(1)} %get-tuple-element.8, s32[256]{0:T(256)S(1)} %get-tuple-element.13, ...), kind=kLoop, calls=%fused_computation.7 | loop fusion | flops 798480 | bytes 17098 | tf_op jit(solution)/shard_map/reduce_sum | solution.py:238
  1.8 61.9 %fetch_multiply_reduce.1 = bf16[2,256,256]{2,1,0:T(8,128)(2,1)} custom-call(s32[3,5,16]{2,1,0:T(8,128)} %fusion.3.index, s32[4]{0:T(128)} %klass.1, s32[2,16]{1,0:T(2,128)} %sizes.1, bf16[16,256,256]{2,1,0:T(8,128)(2,1)} %wf_hbm.1, bf16[4,4,2,2,256,256]{5,4,3,2,1,0:T(8,128)(2,1)} %bitcast.2, bf16[4,4,2,2,256,256]{5,4,3,2,1,0:T(8,128)(2,1)} %bitcast.3), custom_call_target="tpu_custom_call" | custom-call | flops 4294967296 | bytes 18874368 | tf_op jit(solution)/shard_map/fetch_multiply_reduce/pallas_call | solution.py:246
  63.8 1.7 %copy.8 = bf16[2,256,256]{2,1,0:T(8,128)(2,1)} copy(bf16[2,256,256]{2,1,0:T(8,128)(2,1)} %fetch_multiply_reduce.1) | data formatting | bytes 524288
  (5 shorter events, 0.0 us)

commit v3 on v2

--- a/solution.py
+++ b/solution.py
@@ -14,23 +14,26 @@
 TERMS = 4
 CHIP = 2 * TERMS
 
-COOP = ((1, 1), (3, 3), (1, 3), (3, 1), (2, 1), (2, 3), (1, 2), (3, 2), (2, 2))
-DIRECT = ((0, 1), (0, 3), (1, 0), (3, 0), (0, 2), (2, 0))
-OFFSETS = COOP + DIRECT + ((0, 0),)
+PAIR = ((1, 1), (3, 3))
+COOP = (None, (1, 3), (3, 1), (2, 1), (2, 3), (1, 2), (3, 2), (2, 2))
+DIRECT = ((0, 1), (0, 3), (1, 0), (3, 0), (0, 2), (2, 0), None)
+OFFSETS = COOP + DIRECT
 NC, ND, NO = len(COOP), len(DIRECT), len(COOP) + len(DIRECT)
+ALONE = COOP[1:] + DIRECT[:-1] + ((0, 0),)
 UNROLL = 8
+EARLY = 1
 ORDER = (
-    "L0", "L1", "L2", "L3", "L4", "L5", "L6", "L7", "L8", "X0", "T0", "T1", "T2", "T3", "T4", "T5", "D0", "D1", "D2",
-    "D3", "D4", "D5", "S0", "S1", "S2", "S3", "F0", "F1", "S4", "A0", "S5", "F2", "A1", "S6", "F3", "A2", "O0", "P0",
-    "F4", "S7", "A3", "P1", "F5", "S8", "A4", "E0", "P2", "F6", "A5", "E1", "P3", "P4", "F7", "A6", "E2", "E3", "P5",
-    "P9", "F8", "A7", "P6", "P10", "A8", "E4", "E5", "P7", "P11", "P12", "P13", "P14", "P8",
+    "L0", "L1", "L2", "T6", "D6", "T0", "T1", "T2", "T3", "L3", "L4", "D0", "D1", "L5", "L6", "L7", "D2", "D3", "X0",
+    "T4", "T5", "D4", "D5", "S0", "S1", "S2", "F0", "S3", "F1", "A0", "S4", "F2", "A1", "S5", "F3", "A2", "O0", "S6",
+    "P1", "F4", "A3", "P2", "S7", "F5", "A4", "E0", "P3", "F6", "A5", "E1", "P4", "F7", "A6", "E2", "E3", "P5", "P8",
+    "A7", "P6", "P9", "E4", "E5", "E6", "P10", "P11", "P12", "P13", "Q0", "P7",
 )
 
 
 def body(index, klass, sizes, wf_hbm, left_hbm, right_hbm, out, *scratch):
-    recv = scratch[:NO + 1]
-    (wf, left, right, stage_c, stage_d, partial, kept, via_out, via_in, x_out, x_in, kinds_out, kinds_in, kinds,
-     load_sem, ss, rs, sq, rq, sd, rd, sx, rx, sf, rf, sc, rc, sv, rv, sr, rr) = scratch[NO + 1:]
+    fetched = dict(zip(ALONE, scratch))
+    (pair, wf, left, right, stage_c, stage_d, partial, kept, via_out, via_in, x_out, x_in, kinds_out, kinds_in, kinds,
+     load_sem, ss, rs, sq, rq, sd, rd, sx, rx, sf, rf, sc, rc, sv, rv, sr, rr) = scratch[len(ALONE):]
     e, w = lax.axis_index("env"), lax.axis_index("wf")
     x, c, y, z = e // 2, e % 2, w // 4, w % 4
 
@@ -44,7 +47,7 @@
     load_wf = pltpu.make_async_copy(wf_hbm, wf, load_sem.at[0])
     load_wf.start()
     barrier = pltpu.get_barrier_semaphore()
-    partners = [(0, 1, 0, 0), (1, 0, 0, 0), (3, 0, 0, 0)] + [(0, 0, *o) for o in COOP + DIRECT]
+    partners = [(0, 1, 0, 0), (1, 0, 0, 0), (3, 0, 0, 0)] + [(0, 0, *o) for o in ALONE[:-1] + PAIR]
     for p in partners:
         pl.semaphore_signal(barrier, inc=1, device_id=dev(*p), device_id_type=MESH)
     load_wf.wait()
@@ -63,6 +66,16 @@
     next_piece = pl.multiple_of(c * HALF + ((x + 1) % 4) * PIECE, PIECE)
     low = PIECE // 2
 
+    def offset(i):
+        if OFFSETS[i] is None:
+            return (1 + 2 * c,) * 2 if i < NC else (3 - 2 * c,) * 2
+        return OFFSETS[i]
+
+    def blocks(i):
+        if OFFSETS[i] is None:
+            return pair.at[c if i < NC else 1 - c]
+        return fetched[OFFSETS[i]]
+
     def target(o):
         return ((y + o[0]) % 4) * 4 + (z + o[1]) % 4
 
@@ -79,22 +92,22 @@
             dst[k] = masked(wf[q, pl.ds(first, count)], first, q)
 
     def quarter(i):
-        return remote(stage_c.at[i], recv[i].at[:, pl.ds(piece, PIECE)], sq.at[i], rq.at[i], 0, 0, *COOP[i])
+        return remote(stage_c.at[i], blocks(i).at[:, pl.ds(piece, PIECE)], sq.at[i], rq.at[i], 0, 0, *offset(i))
 
     def direct(i):
-        return remote(stage_d.at[i], recv[NC + i].at[:, pl.ds(half, HALF)], sd.at[i], rd.at[i], 0, 0, *DIRECT[i])
+        return remote(stage_d.at[i], blocks(NC + i).at[:, pl.ds(half, HALF)], sd.at[i], rd.at[i], 0, 0, *offset(NC + i))
 
     def share(i, side):
-        part = recv[i].at[:, pl.ds(piece, PIECE)]
+        part = blocks(i).at[:, pl.ds(piece, PIECE)]
         return remote(part, part, sx.at[side, i], rx.at[side, i], 1 if side == 0 else 3, 0, 0, 0)
 
     def forward(i, side):
         first = prev_piece if side == 0 else next_piece + low
-        part = recv[i].at[:, pl.ds(pl.multiple_of(first, low), low)]
+        part = blocks(i).at[:, pl.ds(pl.multiple_of(first, low), low)]
         return remote(part, part, sf.at[side, i], rf.at[side, i], 1 if side == 0 else 3, 0, 0, 0)
 
     def across(i):
-        part = recv[i].at[:, pl.ds(half, HALF)]
+        part = blocks(i).at[:, pl.ds(half, HALF)]
         return remote(part, part, sc.at[i], rc.at[i], 0, 1, 0, 0)
 
     def swap_env(n):
@@ -104,8 +117,7 @@
     def swap_kinds():
         return remote(kinds_out, kinds_in, ss.at[2], rs.at[2], 0, 1, 0, 0)
 
-    def first_product(i):
-        o = OFFSETS[i]
+    def first_product(o, block):
         at = o[0] * 4 + o[1]
 
         @pl.loop(0, CHIP // UNROLL)
@@ -113,11 +125,11 @@
             for u in range(UNROLL):
                 k = n * UNROLL + u
                 q = index[1, kinds[k], at]
-                got = lax.dot_general(left[k, q // 4, q % 2], recv[i][kinds[k]], (((1,), (0,)), ((), ())), preferred_element_type=jnp.float32)
+                got = lax.dot_general(left[k, q // 4, q % 2], block(kinds[k]), (((1,), (0,)), ((), ())), preferred_element_type=jnp.float32)
                 partial[k, at] = got.astype(jnp.bfloat16)
 
-    for i in range(NC):
-        stage(stage_c.at[i], COOP[i], piece, PIECE)
+    for i in range(EARLY):
+        stage(stage_c.at[i], offset(i), piece, PIECE)
     pl.semaphore_wait(barrier, len(partners))
     def step_swap(i):
         swap_kinds().start()
@@ -125,9 +137,11 @@
         swap_env(1).start()
 
     def step_stage(i):
-        stage(stage_d.at[i], DIRECT[i], half, HALF)
+        stage(stage_d.at[i], offset(NC + i), half, HALF)
 
     def step_quarter(i):
+        if i >= EARLY:
+            stage(stage_c.at[i], offset(i), piece, PIECE)
         quarter(i).start()
 
     def step_begin(i):
@@ -154,7 +168,13 @@
 
     def step_product(i):
         across(i).wait_recv()
-        first_product(i)
+        first_product(OFFSETS[i], lambda k: fetched[OFFSETS[i]][k])
+
+    def step_pair(i):
+        across(0).wait_recv()
+        across(NO - 1).wait_recv()
+        for p in range(2):
+            first_product(PAIR[p], lambda k: pair[p, k])
 
     def step_own(i):
         load_left.wait()
@@ -162,10 +182,10 @@
         for k in range(TERMS):
             kinds[(1 - c) * TERMS + k] = kinds_in[k]
         swap_env(0).wait_recv()
-        stage(recv[NO], (0, 0), 0, B)
-        first_product(NO)
-
-    steps = {"L": step_quarter, "X": step_swap, "T": step_stage, "D": step_begin, "S": step_share, "F": step_forward, "A": step_across, "E": step_direct, "P": step_product, "O": step_own}
+        stage(fetched[0, 0], (0, 0), 0, B)
+        first_product((0, 0), lambda k: fetched[0, 0][k])
+
+    steps = {"L": step_quarter, "X": step_swap, "T": step_stage, "D": step_begin, "S": step_share, "F": step_forward, "A": step_across, "E": step_direct, "P": step_product, "Q": step_pair, "O": step_own}
     for step in ORDER:
         steps[step[0]](int(step[1:]))
 
@@ -226,13 +246,13 @@
 
 def shards(wavefunction, left_env, right_env, term_class, sector_sizes, source_table):
     w = lax.axis_index("wf")
-    y, z = w // 4, w % 4
+    y, z = w >> 2, w & 3
     shape = (3, CLASSES, GROUP, GROUP * GROUP)
     what, at, sector = (lax.broadcasted_iota(jnp.int32, shape, n) for n in (0, 2, 3))
-    offset = ((y - source_table // 64) % 4) * 4 + (z - source_table // GROUP % 4) % 4
-    code = (offset * GROUP + source_table % GROUP)[None, :, None, :]
-    offset, place = code // GROUP, code % GROUP
-    group, member = sector // GROUP, sector % GROUP
+    offset = (((y - (source_table >> 6)) & 3) << 2) | ((z - (source_table >> 4)) & 3)
+    code = ((offset << 4) | (source_table & (GROUP - 1)))[None, :, None, :]
+    offset, place = code >> 4, code & (GROUP - 1)
+    group, member = sector >> 4, sector & (GROUP - 1)
     which = jnp.where(what == 0, (group == at) & (offset == 0), (group == w) & (at == jnp.where(what == 1, offset, member)))
     value = jnp.where(what == 0, place, jnp.where(what == 1, member, offset))
     index = jnp.sum(jnp.where(which, value, 0), axis=3)
@@ -248,7 +268,8 @@
         out_shape=jax.ShapeDtypeStruct((2, B, B), bf16),
         in_specs=[smem] * 3 + [anywhere] * 3,
         out_specs=pl.BlockSpec(memory_space=pltpu.VMEM),
-        scratch_shapes=[pltpu.VMEM((CLASSES, B, B), bf16)] * (NO + 1) + [
+        scratch_shapes=[pltpu.VMEM((CLASSES, B, B), bf16)] * len(ALONE) + [
+            pltpu.VMEM((2, CLASSES, B, B), bf16),
             pltpu.VMEM((GROUP, B, B), bf16),
             pltpu.VMEM((CHIP, 4, 2, B, B), bf16),
             pltpu.VMEM((CHIP, 4, 2, B, B), bf16),

time: 65.7 us -> 64.7 us (0.985)
  Pallas kernels: 61.9 us -> 60.2 us
  other arithmetic: 1.8 us -> 2.47 us
    pallas_call x1, Pallas kernels: 61.9 us -> 60.2 us  [shards(): pl.pallas_call(body, out_shape=jax.ShapeDtypeStruct((2, B, B), bf16), in_...]
    and x1 -> x2, other arithmetic: 0.01 us -> 0.72 us  [the longest x1 0.71 us: shards(): offset, place = (code >> 4, code & GROUP - 1)]
where the time goes in v3:
time: 64.7 us; the launch traced here: 64.4 us
  Pallas kernels  60.2 us (93%)
  other arithmetic  2.47 us (4%)
  local copies, waits for them, and re-layouts  1.67 us (3%)
    pallas_call x1, Pallas kernels, shards(): pl.pallas_call(body, out_shape=jax.ShapeDtypeStruct((2, B, B), bf16), in_...  60.2 us
    unnamed x1, local copies, waits for them, and re-layouts  1.67 us

profile of v3, /device:TPU:1, one launch (start us, length us, event | category | flops | bytes accessed | tf_op | source)
XLA Modules:
  0.0 64.4 jit_solution(490009076181664370)
XLA Ops:
  0.0 0.7 %broadcast_and_fusion = s32[5,256]{1,0:T(8,128)S(1)} fusion(s32[5,256]{1,0:T(8,128)} %param.11, s32[]{:T(128)S(6)} %and.42, s32[]{:T(128)S(6)} %shift_right_arithmetic.28), kind=kLoop, calls=%fused_computation.8 | loop fusion | flops 15360 | bytes 10248 | tf_op jit(solution)/shard_map/and | solution.py:254
  0.7 0.7 %broadcast_compare_fusion = (pred[5,256]{1,0:T(8,128)(4,1)S(1)}, s32[5,256]{1,0:T(8,128)S(1)}) fusion(s32[5,256]{1,0:T(8,128)} %param.11, s32[]{:T(128)S(6)} %and.42, s32[]{:T(128)S(6)} %shift_right_arithmetic.28), kind=kLoop, calls=%fused_computation.7 | loop fusion | flops 16640 | bytes 11528 | tf_op jit(solution)/shard_map/eq | solution.py:256
  1.4 1.0 %select_reduce_fusion.index = s32[3,5,16]{2,1,0:T(8,128)} fusion(s32[5,256]{1,0:T(8,128)S(1)} %broadcast_and_fusion, s32[256]{0:T(256)S(1)} %get-tuple-element.7, s32[5,256]{1,0:T(8,128)S(1)} %get-tuple-element.6, s32[256]{0:T(256)S(1)} %get-tuple-element.8, pred[3]{0:T(512)(128)(4,1)S(1)} %get-tuple-element.9, pred[3]{0:T(512)(128)(4,1)S(1)} %get-tuple-element.10, ...), kind=kLoop, calls=%fused_computation | loop fusion | flops 614160 | bytes 14790 | tf_op jit(solution)/shard_map/reduce_sum | solution.py:258
  2.5 60.2 %fetch_multiply_reduce.1 = bf16[2,256,256]{2,1,0:T(8,128)(2,1)} custom-call(s32[3,5,16]{2,1,0:T(8,128)} %select_reduce_fusion.index, s32[4]{0:T(128)} %klass.1, s32[2,16]{1,0:T(2,128)} %sizes.1, bf16[16,256,256]{2,1,0:T(8,128)(2,1)} %wf_hbm.1, bf16[4,4,2,2,256,256]{5,4,3,2,1,0:T(8,128)(2,1)} %bitcast.2, bf16[4,4,2,2,256,256]{5,4,3,2,1,0:T(8,128)(2,1)} %bitcast.3), custom_call_target="tpu_custom_call" | custom-call | flops 4294967296 | bytes 18874368 | tf_op jit(solution)/shard_map/fetch_multiply_reduce/pallas_call | solution.py:266
  62.7 1.7 %copy.8 = bf16[2,256,256]{2,1,0:T(8,128)(2,1)} copy(bf16[2,256,256]{2,1,0:T(8,128)(2,1)} %fetch_multiply_reduce.1) | data formatting | bytes 524288
  (3 shorter events, 0.0 us)

commit v4 on v3

--- a/solution.py
+++ b/solution.py
@@ -23,8 +23,8 @@
 UNROLL = 8
 EARLY = 1
 ORDER = (
-    "L0", "L1", "L2", "T6", "D6", "T0", "T1", "T2", "T3", "L3", "L4", "D0", "D1", "L5", "L6", "L7", "D2", "D3", "X0",
-    "T4", "T5", "D4", "D5", "S0", "S1", "S2", "F0", "S3", "F1", "A0", "S4", "F2", "A1", "S5", "F3", "A2", "O0", "S6",
+    "L0", "L1", "L2", "T6", "D6", "T0", "T1", "T2", "T3", "T4", "T5", "L3", "L4", "D0", "D1", "L5", "L6", "L7", "D2",
+    "D3", "D4", "D5", "X0", "S0", "S1", "S2", "F0", "S3", "F1", "A0", "S4", "F2", "A1", "S5", "F3", "A2", "O0", "S6",
     "P1", "F4", "A3", "P2", "S7", "F5", "A4", "E0", "P3", "F6", "A5", "E1", "P4", "F7", "A6", "E2", "E3", "P5", "P8",
     "A7", "P6", "P9", "E4", "E5", "E6", "P10", "P11", "P12", "P13", "Q0", "P7",
 )
@@ -246,13 +246,13 @@
 
 def shards(wavefunction, left_env, right_env, term_class, sector_sizes, source_table):
     w = lax.axis_index("wf")
-    y, z = w >> 2, w & 3
+    y, z = w // 4, w % 4
     shape = (3, CLASSES, GROUP, GROUP * GROUP)
     what, at, sector = (lax.broadcasted_iota(jnp.int32, shape, n) for n in (0, 2, 3))
-    offset = (((y - (source_table >> 6)) & 3) << 2) | ((z - (source_table >> 4)) & 3)
-    code = ((offset << 4) | (source_table & (GROUP - 1)))[None, :, None, :]
-    offset, place = code >> 4, code & (GROUP - 1)
-    group, member = sector >> 4, sector & (GROUP - 1)
+    offset = ((y - source_table // 64) % 4) * 4 + (z - source_table // GROUP % 4) % 4
+    code = (offset * GROUP + source_table % GROUP)[None, :, None, :]
+    offset, place = code // GROUP, code % GROUP
+    group, member = sector // GROUP, sector % GROUP
     which = jnp.where(what == 0, (group == at) & (offset == 0), (group == w) & (at == jnp.where(what == 1, offset, member)))
     value = jnp.where(what == 0, place, jnp.where(what == 1, member, offset))
     index = jnp.sum(jnp.where(which, value, 0), axis=3)

time: 64.7 us -> 64 us (0.989)
  other arithmetic: 2.47 us -> 1.8 us
    and x2 -> x1, other arithmetic: 0.72 us -> 0.01 us  [shards(): group, member = (sector // GROUP, sector % GROUP)]
where the time goes in v4:
time: 64 us; the launch traced here: 63.7 us
  Pallas kernels  60.2 us (94%)
  other arithmetic  1.8 us (3%)
  local copies, waits for them, and re-layouts  1.67 us (3%)
    pallas_call x1, Pallas kernels, shards(): pl.pallas_call(body, out_shape=jax.ShapeDtypeStruct((2, B, B), bf16), in_...  60.2 us
    unnamed x1, local copies, waits for them, and re-layouts  1.67 us

profile of v4, /device:TPU:1, one launch (start us, length us, event | category | flops | bytes accessed | tf_op | source)
XLA Modules:
  0.0 63.7 jit_solution(9392270829597887169)
XLA Ops:
  0.0 0.7 %broadcast_compare_fusion = (pred[5,256]{1,0:T(8,128)(4,1)S(1)}, s32[5,256]{1,0:T(8,128)S(1)}, s32[5,256]{1,0:T(8,128)S(1)}) fusion(s32[]{:T(128)S(6)} %select_n.88, s32[5,256]{1,0:T(8,128)} %param.11, s32[]{:T(128)S(6)} %select_n.85), kind=kLoop, calls=%fused_computation.48 | loop fusion | flops 107520 | bytes 16648 | tf_op jit(solution)/shard_map/eq | solution.py:256
  0.8 1.0 %fusion.3.index = s32[3,5,16]{2,1,0:T(8,128)} fusion(s32[5,256]{1,0:T(8,128)S(1)} %add_select_fusion, s32[256]{0:T(256)S(1)} %get-tuple-element.9, s32[256]{0:T(256)S(1)} %get-tuple-element.12, s32[5,256]{1,0:T(8,128)S(1)} %get-tuple-element.6, s32[]{:T(128)S(6)} %axis_index.12, s32[256]{0:T(256)S(1)} %get-tuple-element.8, s32[256]{0:T(256)S(1)} %get-tuple-element.13, ...), kind=kLoop, calls=%fused_computation.7 | loop fusion | flops 798480 | bytes 17098 | tf_op jit(solution)/shard_map/reduce_sum | solution.py:258
  1.8 60.2 %fetch_multiply_reduce.1 = bf16[2,256,256]{2,1,0:T(8,128)(2,1)} custom-call(s32[3,5,16]{2,1,0:T(8,128)} %fusion.3.index, s32[4]{0:T(128)} %klass.1, s32[2,16]{1,0:T(2,128)} %sizes.1, bf16[16,256,256]{2,1,0:T(8,128)(2,1)} %wf_hbm.1, bf16[4,4,2,2,256,256]{5,4,3,2,1,0:T(8,128)(2,1)} %bitcast.2, bf16[4,4,2,2,256,256]{5,4,3,2,1,0:T(8,128)(2,1)} %bitcast.3), custom_call_target="tpu_custom_call" | custom-call | flops 4294967296 | bytes 18874368 | tf_op jit(solution)/shard_map/fetch_multiply_reduce/pallas_call | solution.py:266
  62.0 1.7 %copy.8 = bf16[2,256,256]{2,1,0:T(8,128)(2,1)} copy(bf16[2,256,256]{2,1,0:T(8,128)(2,1)} %fetch_multiply_reduce.1) | data formatting | bytes 524288
  (5 shorter events, 0.0 us)
